TPU v7x, 32 devices: a whole 2x2x4 slice. The times are simulated.
32 devices in a mesh: parts: 2 (over y), row: 4 (over z), dim: 4 (over x, core).
Axes of the slice: x: 2, y: 2, z: 4, core: 2. Of those that a mesh axis runs over, the one named last changes fastest.
Arguments:
- train_grads: bfloat16 [8192, 8192], P(('parts', 'row'), 'dim'), parts along dimension 0, may hold values from -16 to 16
- precond: float32 [8192], P('dim'), may hold values from 0.25 to 20
- query_store: bfloat16 [8, 256, 8192], P(('parts', 'row'), None, 'dim'), parts along dimension 0, may hold values from -16 to 16
- owner: int32 [8], P('parts'), parts along dimension 0, may hold values from 0 to 3, as said below
- order: int32 [8], P('parts'), parts along dimension 0, may hold values from 0 to 3, each once
Outputs:
- scores: float32 [4, 8192, 256], P(None, ('parts', 'row', 'dim')), parts along dimension 1
There are 2 independent parts, one for each index of `parts`. A program takes and returns all parts, laid end to end along the dimension named above; an argument that names none is the same for every part. Nothing has to cross between parts.
Inputs may be any that keep to these rules, and one draw needn't show every extreme that they name: `owner`: distinct slots; slot 0 and slot 3 each hold one of the blocks.
All inputs are finite; a program needn't handle non-finite values.
Results may differ from a plain program's by a relative error of at most 0.008.
Values may be sent and summed in bfloat16 or wider, within the bound.
A program may use at most 64 MiB of HBM per device.

v0:
```python
import jax
import jax.numpy as jnp
from jax import lax
from jax.sharding import PartitionSpec as P

K = 8192
NB = 4


def broadcast(value, axis, source):
    kept = jnp.where(lax.axis_index(axis) == source, value, 0).astype(value.dtype)
    return lax.psum(kept, axis)


def weighted_norm(values, precond):
    wide = values.astype(jnp.float32)
    return jnp.sum(wide * wide * precond[None, :], axis=1) / K


def on_device(train_grads, precond, query_store, owner, order):
    rows = train_grads.shape[0]
    share = rows // lax.axis_size("dim")
    slot = query_store[0]
    local_gsq = weighted_norm(train_grads, precond)
    gsq = lax.psum(local_gsq, "dim")
    own_gsq = lax.dynamic_slice_in_dim(gsq, lax.axis_index("dim") * share, share)
    norm_list = []
    results = []
    for step in range(NB):
        root = owner[order[step]]
        block = broadcast(slot, "row", root)
        qsq = lax.psum(weighted_norm(block, precond), "dim")
        weighted = (block.astype(jnp.float32) * precond[None, :]).astype(jnp.bfloat16)

        def product(start, count, weighted=weighted):
            return lax.dot_general(
                train_grads, weighted, (((1,), (1,)), ((), ())), preferred_element_type=jnp.float32
            )

        norm_list.append(qsq)
        summed = lax.psum_scatter(
            product(jnp.int32(0), share * lax.axis_size("dim")).astype(jnp.bfloat16),
            "dim",
            scatter_dimension=0,
            tiled=True,
        ).astype(jnp.float32)
        results.append(summed / jnp.sqrt(K * (own_gsq[:, None] + 1e-06) * (qsq[None, :] + 1e-06)))
    return jnp.stack(results)


def solution(mesh):
    return jax.shard_map(
        on_device,
        mesh=mesh,
        in_specs=(
            P(("parts", "row"), "dim"),
            P("dim"),
            P(("parts", "row"), None, "dim"),
            P("parts"),
            P("parts"),
        ),
        out_specs=P(None, ("parts", "row", "dim"), None),
        check_vma=False,
    )
```

profile of v0, /device:TPU:1, one launch (start us, length us, event | category | flops | bytes accessed | tf_op | source)
XLA Modules:
  0.0 288.6 jit_solution(7581045500723188570)
XLA Ops:
  6.5 1.5 fusion.25
  15.6 1.5 fusion.24
  19.6 3.3 %select_bitcast_fusion.1 = (bf16[256,2048]{1,0:T(8,128)(2,1)}, bf16[256,2048]{1,0:T(8,128)(2,1)}, bf16[256,2048]{1,0:T(8,128)(2,1)}, bf16[256,2048]{1,0:T(8,128)(2,1)}) fusion(bf16[1,256,2048]{2,1,0:T(8,128)(2,1)} %param.7, pred[]{:T(512)S(6)} %eq.14, pred[]{:T(512)S(6)} %eq.13, pred[]{:T(512)S(6)} %eq.12, pred[]{:T(512)S(6)} %eq.15), kind=kLoop, calls=%fused_computation.31 | loop fusion | flops 2097152 | bytes 5242884 | tf_op jit(solution)/shard_map/jit(_where)/select_n | solution.py:11
  23.0 0.0 reduce-scatter.11.cloned.1.call-start
  23.0 158.2 %all-reduce.4.cloned.1.call-done = (bf16[256,2048]{1,0:T(8,128)(2,1)}, bf16[256,2048]{1,0:T(8,128)(2,1)}, bf16[256,2048]{1,0:T(8,128)(2,1)}, bf16[256,2048]{1,0:T(8,128)(2,1)}) async-done(((bf16[256,2048]{1,0:T(8,128)(2,1)}, bf16[256,2048]{1,0:T(8,128)(2,1)}, bf16[256,2048]{1,0:T(8,128)(2,1)}, bf16[256,2048]{1,0:T(8,128)(2,1)}), (bf16[256,2048]{1,0:T(8,128)(2,1)}, bf16[256,2048]{1,0:T(8,128)(2,1)}, ...) | async-done | bytes 4194320 | tf_op jit(solution)/shard_map/psum | solution.py:12
  181.3 4.7 %fusion.15 = bf16[1024,256]{0,1:T(8,128)(2,1)} fusion(bf16[1024,2048]{1,0:T(8,128)(2,1)} %param.5, bf16[256,2048]{1,0:T(8,128)(2,1)} %get-tuple-element.14, f32[2048]{0:T(1024)S(1)} %copy-done.5), kind=kOutput, calls=%fused_computation.28 | convolution fusion | flops 1075576832 | bytes 5775360 | tf_op jit(solution)/shard_map/dot_general | solution.py:36
  186.0 0.0 reduce-scatter.5.cloned.1.call-start
  186.0 4.3 %fusion.12 = bf16[1024,256]{0,1:T(8,128)(2,1)} fusion(bf16[1024,2048]{1,0:T(8,128)(2,1)} %param.5, bf16[256,2048]{1,0:T(8,128)(2,1)S(1)} %copy-done.4, f32[2048]{0:T(1024)S(1)} %copy-done.5), kind=kOutput, calls=%fused_computation.25 | convolution fusion | flops 1075576832 | bytes 5775360 | tf_op jit(solution)/shard_map/dot_general | solution.py:36
  190.3 0.0 reduce-scatter.7.cloned.1.call-start
  190.4 3.6 %multiply_reduce_fusion = f32[1024]{0:T(1024)S(1)} fusion(bf16[1024,2048]{1,0:T(8,128)(2,1)} %param.5, f32[2048]{0:T(1024)S(1)} %copy-done.5), kind=kLoop, calls=%fused_computation | loop fusion | flops 8387584 | bytes 4206592 | tf_op jit(solution)/shard_map/reduce_sum | solution.py:17
  194.0 0.0 copy-done
  194.0 3.4 %fusion.13 = bf16[1024,256]{0,1:T(8,128)(2,1)} fusion(bf16[1024,2048]{1,0:T(8,128)(2,1)S(1)} %copy-done, bf16[256,2048]{1,0:T(8,128)(2,1)} %get-tuple-element.16, f32[2048]{0:T(1024)S(1)} %copy-done.5), kind=kOutput, calls=%fused_computation.26 | convolution fusion | flops 1075576832 | bytes 5775360 | tf_op jit(solution)/shard_map/dot_general | solution.py:36
  197.5 0.0 reduce-scatter.9.cloned.1.call-start
  197.6 2.5 fusion.2
  200.1 2.1 fusion.14
  202.3 5.8 %all-reduce = (f32[256]{0:T(256)S(1)}, f32[1024]{0:T(1024)S(1)}, f32[256]{0:T(256)S(1)}, f32[256]{0:T(256)S(1)}, f32[256]{0:T(256)S(1)}) all-reduce(f32[256]{0:T(256)S(1)} %get-tuple-element.34, f32[1024]{0:T(1024)S(1)} %broadcast_multiply_fusion, f32[256]{0:T(256)S(1)} %get-tuple-element.35, ...), channel_id=1, replica_groups=mesh['parts'=2,'row'=4,'dim'=4] {'dim'}, use_global_device_ids=true, to_apply=%region_17.18 | all-reduce | flops 2048 | bytes 16384 | tf_op jit(solution)/shard_map/psum | solution.py:32
  208.1 0.1 add_multiply_fusion
  208.2 0.0 reduce-scatter.11.cloned.1.call-done
  208.2 22.9 %reduce-scatter.5.cloned.1.call-done = bf16[256,256]{0,1:T(8,128)(2,1)} async-done(((bf16[1024,256]{0,1:T(8,128)(2,1)}), bf16[256,256]{0,1:T(8,128)(2,1)}) %reduce-scatter.5.cloned.1.call-update) | async-done | bytes 131088 | tf_op jit(solution)/shard_map/reduce_scatter | solution.py:41
  231.1 24.2 %reduce-scatter.7.cloned.1.call-done = bf16[256,256]{0,1:T(8,128)(2,1)} async-done(((bf16[1024,256]{0,1:T(8,128)(2,1)}), bf16[256,256]{0,1:T(8,128)(2,1)}) %reduce-scatter.7.cloned.1.call-update) | async-done | bytes 131088 | tf_op jit(solution)/shard_map/reduce_scatter | solution.py:41
  255.3 24.0 %reduce-scatter.9.cloned.1.call-done = bf16[256,256]{0,1:T(8,128)(2,1)} async-done(((bf16[1024,256]{0,1:T(8,128)(2,1)}), bf16[256,256]{0,1:T(8,128)(2,1)}) %reduce-scatter.9.cloned.1.call-update) | async-done | bytes 131088 | tf_op jit(solution)/shard_map/reduce_scatter | solution.py:41
  279.3 1.3 multiply_bitcast_fusion.3
  280.6 0.1 pad_maximum_fusion
  280.7 1.3 copy.6
  (24 shorter events, 0.1 us)
Async XLA Ops:
  6.5 174.7 %all-reduce.4.cloned.1.call-start = ((), (), s32[]{:S(2)}) async-start(), calls=%async_computation.8 | async-start | bytes 8388608 | tf_op jit(solution)/shard_map/psum | solution.py:12
  23.0 158.3 %copy-start.5 = (f32[2048]{0:T(1024)S(1)}, f32[2048]{0:T(1024)}, u32[]{:S(2)}) copy-start(f32[2048]{0:T(1024)} %param.6) | copy-start | bytes 24580
  23.0 185.2 %reduce-scatter.11.cloned.1.call-start = ((), (), s32[]{:S(2)}) async-start(), calls=%async_computation.7 | async-start | bytes 655360 | tf_op jit(solution)/shard_map/reduce_scatter | solution.py:41
  181.3 4.8 %copy-start.4 = (bf16[256,2048]{1,0:T(8,128)(2,1)S(1)}, bf16[256,2048]{1,0:T(8,128)(2,1)}, u32[]{:S(2)}) copy-start(bf16[256,2048]{1,0:T(8,128)(2,1)} %get-tuple-element.15) | copy-start | bytes 3145732
  186.0 45.2 %reduce-scatter.5.cloned.1.call-start = ((), (), s32[]{:S(2)}) async-start(), calls=%async_computation.4 | async-start | bytes 655360 | tf_op jit(solution)/shard_map/reduce_scatter | solution.py:41
  190.3 65.0 %reduce-scatter.7.cloned.1.call-start = ((), (), s32[]{:S(2)}) async-start(), calls=%async_computation.5 | async-start | bytes 655360 | tf_op jit(solution)/shard_map/reduce_scatter | solution.py:41
  190.4 3.6 %copy-start = (bf16[1024,2048]{1,0:T(8,128)(2,1)S(1)}, bf16[1024,2048]{1,0:T(8,128)(2,1)}, u32[]{:S(2)}) copy-start(bf16[1024,2048]{1,0:T(8,128)(2,1)} %param.5) | copy-start | bytes 12582916
  194.0 3.5 %copy-start.2 = (bf16[256,2048]{1,0:T(8,128)(2,1)S(1)}, bf16[256,2048]{1,0:T(8,128)(2,1)}, u32[]{:S(2)}) copy-start(bf16[256,2048]{1,0:T(8,128)(2,1)} %get-tuple-element.17) | copy-start | bytes 3145732
  194.0 3.5 %copy-start.3 = (bf16[256,2048]{1,0:T(8,128)(2,1)S(1)}, bf16[256,2048]{1,0:T(8,128)(2,1)}, u32[]{:S(2)}) copy-start(bf16[256,2048]{1,0:T(8,128)(2,1)} %get-tuple-element.14) | copy-start | bytes 3145732
  197.5 81.9 %reduce-scatter.9.cloned.1.call-start = ((), (), s32[]{:S(2)}) async-start(), calls=%async_computation.6 | async-start | bytes 655360 | tf_op jit(solution)/shard_map/reduce_scatter | solution.py:41
  197.5 2.6 copy-start.1
Sparse Core Ops, SparseCore 0:
  23.1 158.0 all-reduce.3
  186.1 20.6 reduce-scatter.10
  209.2 21.8 reduce-scatter.4
  233.6 21.6 reduce-scatter.6
  257.6 21.6 reduce-scatter.8
where the time goes:
time: 290 us; the launch traced here: 289 us
  waiting for transfers between devices  229 us (79%)
  between operations  23.4 us (8%)
  matrix products  14.5 us (5%)
  other arithmetic  10.9 us (4%)
  blocking collectives  5.79 us (2%)
  local copies, waits for them, and re-layouts  4.31 us (1%)
    psum x1, waiting for transfers between devices, broadcast(): return lax.psum(kept, axis)  158 us
    reduce_scatter x4, waiting for transfers between devices, on_device(): lax.psum_scatter(product(jnp.int32(0), share * lax.axis_size('dim')).asty...  71.2 us
    dot_general x4, matrix products, product(): lax.dot_general(train_grads, weighted, (((1,), (1,)), ((), ())), preferre...  14.5 us
    reduce_sum x2, other arithmetic, weighted_norm(): return jnp.sum(wide * wide * precond[None, :], axis=1) / K  6.11 us
  transfers between devices with their start and end apart: 5, of which 4 were waited for; matrix products, arithmetic and copies ran while one was open for 6% of the time, Pallas kernels for 0%

commit v1 on v0

v1 whole, which is shorter than its diff:
```python
import functools

import jax
import jax.numpy as jnp
from jax import lax
from jax.experimental import pallas as pl
from jax.experimental.pallas import tpu as pltpu
from jax.sharding import PartitionSpec as P

K = 8192
NB = 4
CHUNK = 64
AHEAD = 2
MESH = pl.DeviceIdType.MESH
NT = (((1,), (1,)), ((), ()))


def row_sums(values, precond):
    wide = values.astype(jnp.float32)
    squares = wide * wide * precond
    lanes = squares[:, :128]
    for at in range(128, squares.shape[1], 128):
        lanes = lanes + squares[:, at : at + 128]
    return jnp.sum(lanes.T, axis=0, keepdims=True)


def score_kernel(
    n_row, n_dim, train_hbm, precond_ref, slot_hbm, raw_ref, g_ref, q_ref,
    train, slot, blocks, parts, landed, g_out, g_in, q_out, q_in, q_sum, q_all,
    load_sem, hop_send, hop_recv, part_send, part_recv, norm_send, norm_recv, q_send, q_recv,
):
    z = lax.axis_index("row")
    d = lax.axis_index("dim")
    rows = train.shape[0]
    queries = slot.shape[0]
    share = rows // n_dim
    steps = queries // CHUNK
    half = 2 * CHUNK

    load_slot = pltpu.make_async_copy(slot_hbm, slot, load_sem.at[0])
    load_train = pltpu.make_async_copy(train_hbm, train, load_sem.at[1])
    load_slot.start()
    load_train.start()

    barrier = pltpu.get_barrier_semaphore()
    for r in range(1, n_row):
        pl.semaphore_signal(barrier, inc=1, device_id={"row": lax.rem(z + r, n_row)}, device_id_type=MESH)
    for r in range(1, n_dim):
        pl.semaphore_signal(barrier, inc=1, device_id={"dim": lax.rem(d + r, n_dim)}, device_id_type=MESH)

    def rows_of(c):
        return pl.ds(pl.multiple_of(c * CHUNK, CHUNK), CHUNK)

    def hop(way, b, c):
        to = z + 1 if way == 0 else z - 1
        piece = blocks.at[b, rows_of(c)]
        return pltpu.make_async_remote_copy(
            src_ref=piece, dst_ref=piece, send_sem=hop_send.at[way, b, c], recv_sem=hop_recv.at[b, c],
            device_id={"row": to}, device_id_type=MESH,
        )

    def send_part(b, c, r):
        to = lax.rem(d + r, n_dim)
        return pltpu.make_async_remote_copy(
            src_ref=parts.at[b, to, rows_of(c)], dst_ref=landed.at[b, d, rows_of(c)],
            send_sem=part_send.at[b, r, c], recv_sem=part_recv.at[b, r, c],
            device_id={"dim": to}, device_id_type=MESH,
        )

    def weigh(c):
        blocks[z, rows_of(c), :] = (slot[rows_of(c), :].astype(jnp.float32) * precond_ref[...]).astype(jnp.bfloat16)

    def send_own(c):
        pl.when(z < n_row - 1)(lambda: hop(0, z, c).start())
        pl.when(z > 0)(lambda: hop(1, z, c).start())

    def product(b, c):
        weighted = blocks[b, rows_of(c), :]
        for r in PART_ORDER(n_dim):
            to = lax.rem(d + r, n_dim)
            mine = train[pl.ds(pl.multiple_of(to * share, share), share), :]
            part = lax.dot_general(weighted, mine, NT, preferred_element_type=jnp.float32)
            parts[b, to, rows_of(c), :] = part.astype(jnp.bfloat16)
            if r:
                send_part(b, c, r).start()

    def add_up(b, which):
        for k in range(2):
            for r in range(1, n_dim):
                send_part(b, which * 2 + k, r).wait_recv()
        at = pl.ds(which * half, half)
        total = parts[b, d, at, :].astype(jnp.float32)
        for r in range(1, n_dim):
            total = total + landed[b, lax.rem(d + r, n_dim), at, :].astype(jnp.float32)
        raw_ref[b, :, at] = total.T

    def each_block(h, run):
        if h == 0:
            run(z)
        elif h < n_row:
            pl.when(z - h >= 0)(lambda: run(z - h))
            pl.when(z + h < n_row)(lambda: run(z + h))

    load_slot.wait()
    for c in range(AHEAD):
        weigh(c)
    pl.semaphore_wait(barrier, n_row - 1 + n_dim - 1)
    for c in range(AHEAD):
        send_own(c)
    for c in range(AHEAD, steps):
        weigh(c)

    q_out[...] = jnp.broadcast_to(row_sums(slot[...], precond_ref[...]), q_out.shape)

    def norm_copy(r, which):
        to = lax.rem(d + r, n_dim)
        src, dst = (g_out.at[to], g_in.at[d]) if which == 0 else (q_out, q_in.at[d])
        return pltpu.make_async_remote_copy(
            src_ref=src, dst_ref=dst, send_sem=norm_send.at[which, r], recv_sem=norm_recv.at[which, r],
            device_id={"dim": to}, device_id_type=MESH,
        )

    def q_copy(r):
        return pltpu.make_async_remote_copy(
            src_ref=q_sum, dst_ref=q_all.at[z], send_sem=q_send.at[r], recv_sem=q_recv.at[r],
            device_id={"row": lax.rem(z + r, n_row)}, device_id_type=MESH,
        )

    for r in range(1, n_dim):
        norm_copy(r, 1).start()
    load_train.wait()

    def train_norms(t):
        at = pl.ds(pl.multiple_of(t * share, share), share)
        g_out[t] = jnp.broadcast_to(row_sums(train[at, :], precond_ref[...]), g_out.shape[1:])

    for h in range(1, n_row):

        def step(c, carry, h=h):
            def arrive_left():
                hop(0, z - h, c).wait_recv()
                pl.when(z < n_row - 1)(lambda: hop(0, z - h, c).start())

            def arrive_right():
                hop(1, z + h, c).wait_recv()
                pl.when(z > 0)(lambda: hop(1, z + h, c).start())

            if h == 1:
                product(z, c)
            pl.when(z - h >= 0)(arrive_left)
            pl.when(z + h < n_row)(arrive_right)
            if h == 1:
                pl.when(c + AHEAD < steps)(lambda: send_own(c + AHEAD))
            each_block(h, lambda b: product(b, c))
            for which in range(steps // 2):
                if which == 0:
                    pl.when(c == 0)(lambda: each_block(h - 1, lambda b: add_up(b, steps // 2 - 1)) if h > 1 else None)
                else:
                    pl.when(c == 2 * which)(lambda which=which: each_block(h, lambda b: add_up(b, which - 1)))
            if h == 1:
                pl.when(c < n_dim)(lambda: train_norms(c))
            return carry

        lax.fori_loop(0, steps, step, 0)
        if h == 1:
            for t in range(steps, n_dim):
                train_norms(t)
            for r in range(1, n_dim):
                norm_copy(r, 0).start()
            for r in range(1, n_dim):
                norm_copy(r, 1).wait_recv()
            total = q_out[...]
            for r in range(1, n_dim):
                total = total + q_in[lax.rem(d + r, n_dim)]
            q_sum[...] = total
            q_ref[z] = total
            for r in range(1, n_row):
                q_copy(r).start()
            for which in range(steps // 2):
                add_up(z, which)
            for r in range(1, n_dim):
                norm_copy(r, 0).wait_recv()
            total = g_out[d]
            for r in range(1, n_dim):
                total = total + g_in[lax.rem(d + r, n_dim)]
            g_ref[...] = total
        if h == 2:
            for r in range(1, n_row):
                q_copy(r).wait_recv()
            for r in range(1, n_row):
                other = lax.rem(z + r, n_row)
                q_ref[other] = q_all[other]
    each_block(n_row - 1, lambda b: add_up(b, steps // 2 - 1))

    def sent(c, carry):
        for b in range(n_row):
            pl.when((z < n_row - 1) & (b <= z))(lambda b=b: hop(0, b, c).wait_send())
            pl.when((z > 0) & (b >= z))(lambda b=b: hop(1, b, c).wait_send())
            for r in range(1, n_dim):
                send_part(b, c, r).wait_send()
        return carry

    lax.fori_loop(0, steps, sent, 0)
    for r in range(1, n_dim):
        norm_copy(r, 0).wait_send()
        norm_copy(r, 1).wait_send()
    for r in range(1, n_row):
        q_copy(r).wait_send()


def PART_ORDER(n_dim):
    middle = n_dim // 2
    return [middle] + [r for r in range(1, n_dim) if r != middle] + [0]


def raw_scores(n_row, n_dim, train_grads, precond, slot):
    rows, width = train_grads.shape
    queries = slot.shape[0]
    share = rows // n_dim
    steps = queries // CHUNK
    f32, bf16 = jnp.float32, jnp.bfloat16
    vmem = pl.BlockSpec(memory_space=pltpu.VMEM)
    anywhere = pl.BlockSpec(memory_space=pl.ANY)
    dma = pltpu.SemaphoreType.DMA
    return pl.pallas_call(
        functools.partial(score_kernel, n_row, n_dim),
        out_shape=(
            jax.ShapeDtypeStruct((n_row, share, queries), f32),
            jax.ShapeDtypeStruct((8, share), f32),
            jax.ShapeDtypeStruct((n_row, 8, queries), f32),
        ),
        in_specs=[anywhere, vmem, anywhere],
        out_specs=(vmem, vmem, vmem),
        scratch_shapes=[
            pltpu.VMEM((rows, width), bf16),
            pltpu.VMEM((queries, width), bf16),
            pltpu.VMEM((n_row, queries, width), bf16),
            pltpu.VMEM((n_row, n_dim, queries, share), bf16),
            pltpu.VMEM((n_row, n_dim, queries, share), bf16),
            pltpu.VMEM((n_dim, 8, share), f32),
            pltpu.VMEM((n_dim, 8, share), f32),
            pltpu.VMEM((8, queries), f32),
            pltpu.VMEM((n_dim, 8, queries), f32),
            pltpu.VMEM((8, queries), f32),
            pltpu.VMEM((n_row, 8, queries), f32),
            dma((2,)),
            dma((2, n_row, steps)),
            dma((n_row, steps)),
            dma((n_row, n_dim, steps)),
            dma((n_row, n_dim, steps)),
            dma((2, n_dim)),
            dma((2, n_dim)),
            dma((n_row,)),
            dma((n_row,)),
        ],
        compiler_params=pltpu.CompilerParams(
            collective_id=0, has_side_effects=True, vmem_limit_bytes=48 * 1024 * 1024
        ),
        name="scores_raw",
    )(train_grads, precond.reshape(1, width), slot)


def normalise_kernel(owner, order, raw_ref, g_ref, q_ref, out_ref):
    queries = raw_ref.shape[2]
    share = raw_ref.shape[1]
    g = lax.rsqrt(K * (g_ref[0:1, :] / K + 1e-06))
    column = jnp.broadcast_to(g, (128, share)).T
    q = lax.rsqrt(q_ref[0, 0:1, :] / K + 1e-06)
    for at in range(0, queries, 128):
        out_ref[0, :, at : at + 128] = raw_ref[0, :, at : at + 128] * column * q[:, at : at + 128]


def normalise(raw, g, q, owner, order):
    n, share, queries = raw.shape
    return pl.pallas_call(
        normalise_kernel,
        out_shape=jax.ShapeDtypeStruct((NB, share, queries), jnp.float32),
        grid_spec=pltpu.PrefetchScalarGridSpec(
            num_scalar_prefetch=2,
            grid=(NB,),
            in_specs=[
                pl.BlockSpec((1, share, queries), lambda s, owner, order: (owner[order[s]], 0, 0)),
                pl.BlockSpec((8, share), lambda s, owner, order: (0, 0)),
                pl.BlockSpec((1, 8, queries), lambda s, owner, order: (owner[order[s]], 0, 0)),
            ],
            out_specs=pl.BlockSpec((1, share, queries), lambda s, owner, order: (s, 0, 0)),
        ),
        name="normalise",
    )(owner, order, raw, g, q)


def every_slot(train_grads, precond, query_store, owner, order):
    raw, g, q = raw_scores(lax.axis_size("row"), lax.axis_size("dim"), train_grads, precond, query_store[0])
    return normalise(raw, g, q, owner, order)


def weighted_norm(values, precond):
    wide = values.astype(jnp.float32)
    return jnp.sum(wide * wide * precond[None, :], axis=1) / K


def some_slots(train_grads, precond, query_store, owner, order):
    share = train_grads.shape[0] // lax.axis_size("dim")
    slot = query_store[0]
    roots = owner[order]
    mine = (roots == lax.axis_index("row"))[:, None, None]
    blocks = lax.psum(jnp.where(mine, slot[None], 0).astype(jnp.bfloat16), "row")
    gsq = lax.psum_scatter(weighted_norm(train_grads, precond), "dim", tiled=True)
    results = []
    for step in range(NB):
        block = blocks[step]
        qsq = lax.psum(weighted_norm(block, precond), "dim")
        weighted = (block.astype(jnp.float32) * precond[None, :]).astype(jnp.bfloat16)
        part = lax.dot_general(train_grads, weighted, NT, preferred_element_type=jnp.float32)
        summed = lax.psum_scatter(part.astype(jnp.bfloat16), "dim", scatter_dimension=0, tiled=True)
        scale = jnp.sqrt(K * (gsq[:, None] + 1e-06) * (qsq[None, :] + 1e-06))
        results.append(summed.astype(jnp.float32) / scale)
    return jnp.stack(results)


def solution(mesh):
    return jax.shard_map(
        every_slot if mesh.shape["row"] == NB else some_slots,
        mesh=mesh,
        in_specs=(
            P(("parts", "row"), "dim"),
            P("dim"),
            P(("parts", "row"), None, "dim"),
            P("parts"),
            P("parts"),
        ),
        out_specs=P(None, ("parts", "row", "dim"), None),
        check_vma=False,
    )
```

time: 290 us -> 89.5 us (0.31)
  waiting for transfers between devices: 229 us -> 0 us
  Pallas kernels: 0 us -> 85.1 us
  between operations: 23.4 us -> 0.02 us
  matrix products: 14.5 us -> 0 us
  other arithmetic: 10.9 us -> 0 us
  blocking collectives: 5.79 us -> 0 us
    psum x1 -> x0, waiting for transfers between devices: 158 us -> none  [broadcast(): return lax.psum(kept, axis)]
    pallas_call x0 -> x2, Pallas kernels: none -> 85.1 us  [the longest x1 80.8 us: raw_scores(): pl.pallas_call(functools.partial(score_kernel, n_row, n_dim), out_shape=(...]
    reduce_scatter x4 -> x0, waiting for transfers between devices: 71.2 us -> none  [on_device(): lax.psum_scatter(product(jnp.int32(0), share * lax.axis_size('dim')).asty...]
    dot_general x4 -> x0, matrix products: 14.5 us -> none  [product(): lax.dot_general(train_grads, weighted, (((1,), (1,)), ((), ())), preferre...]
    reduce_sum x2 -> x0, other arithmetic: 6.11 us -> none  [weighted_norm(): return jnp.sum(wide * wide * precond[None, :], axis=1) / K]
    psum x1 -> x0, blocking collectives: 5.79 us -> none  [on_device(): qsq = lax.psum(weighted_norm(block, precond), 'dim')]
    unnamed x12 -> x10, local copies, waits for them, and re-layouts: 0.06 us -> 4.08 us
    select_n x1 -> x0, other arithmetic: 3.34 us -> none  [broadcast(): jnp.where(lax.axis_index(axis) == source, value, 0).astype(value.dtype)]
  transfers between devices with their start and end apart: 5 -> 0, of which waited for: 4 -> 0; matrix products, arithmetic and copies ran while one was open for 6% -> 0% of each run, Pallas kernels for 0% -> 0%
where the time goes in v1:
time: 89.5 us; the launch traced here: 89.2 us
  Pallas kernels  85.1 us (95%)
  local copies, waits for them, and re-layouts  4.08 us (5%)
    pallas_call x1, Pallas kernels, raw_scores(): pl.pallas_call(functools.partial(score_kernel, n_row, n_dim), out_shape=(...  80.8 us
    pallas_call x1, Pallas kernels, normalise(): pl.pallas_call(normalise_kernel, out_shape=jax.ShapeDtypeStruct((NB, shar...  4.25 us
    unnamed x10, local copies, waits for them, and re-layouts  4.08 us

profile of v1, /device:TPU:1, one launch (start us, length us, event | category | flops | bytes accessed | tf_op | source)
XLA Modules:
  0.0 89.2 jit_solution(13266724841748661706)
XLA Ops:
  0.0 0.0 copy-start
  0.0 1.2 %copy-done = bf16[1,256,2048]{2,1,0:T(8,128)(2,1)S(1)} copy-done((bf16[1,256,2048]{2,1,0:T(8,128)(2,1)S(1)}, bf16[1,256,2048]{2,1,0:T(8,128)(2,1)}, u32[]{:S(2)}) %copy-start) | copy-done | bytes 1048600
  1.2 0.0 copy-start.3
  1.2 0.7 copy-done.3
  1.9 80.8 %scores_raw.1 = (f32[4,256,256]{2,1,0:T(8,128)S(1)}, f32[8,256]{1,0:T(8,128)S(1)}, f32[4,8,256]{2,1,0:T(8,128)S(1)}) custom-call(bf16[1024,2048]{1,0:T(8,128)(2,1)} %train_hbm.1, f32[1,2048]{1,0:T(1,128)S(1)} %bitcast.3, bf16[256,2048]{1,0:T(8,128)(2,1)S(1)} %bitcast.2), custom_call_target="tpu_custom_call" | custom-call | tf_op jit(solution)/shard_map/scores_raw/pallas_call | solution.py:225
  82.8 0.0 copy-start.1
  82.8 1.0 %copy-done.1 = f32[4,256,256]{2,1,0:T(8,128)} copy-done((f32[4,256,256]{2,1,0:T(8,128)}, f32[4,256,256]{2,1,0:T(8,128)S(1)}, u32[]{:S(2)}) %copy-start.1) | copy-done | bytes 1048600
  83.8 0.0 copy-start.2
  83.8 0.6 copy-done.2
  84.4 0.0 copy-start.4
  84.4 0.6 copy-done.4
  85.0 4.2 %normalise.1 = f32[4,256,256]{2,1,0:T(8,128)} custom-call(s32[4]{0:T(128)} %owner.1, s32[4]{0:T(128)} %order.1, f32[4,256,256]{2,1,0:T(8,128)} %copy-done.1, f32[8,256]{1,0:T(8,128)} %copy-done.4, f32[4,8,256]{2,1,0:T(8,128)} %copy-done.2), custom_call_target="tpu_custom_call" | custom-call | tf_op jit(solution)/shard_map/normalise/pallas_call | solution.py:275
Async XLA Ops:
  0.0 1.2 %copy-start = (bf16[1,256,2048]{2,1,0:T(8,128)(2,1)S(1)}, bf16[1,256,2048]{2,1,0:T(8,128)(2,1)}, u32[]{:S(2)}) copy-start(bf16[1,256,2048]{2,1,0:T(8,128)(2,1)} %param.7) | copy-start | bytes 3145732
  1.2 0.7 copy-start.3
  82.8 1.0 %copy-start.1 = (f32[4,256,256]{2,1,0:T(8,128)}, f32[4,256,256]{2,1,0:T(8,128)S(1)}, u32[]{:S(2)}) copy-start(f32[4,256,256]{2,1,0:T(8,128)S(1)} %get-tuple-element.8.raw_ref) | copy-start | bytes 3145732
  83.8 0.6 copy-start.2
  84.4 0.6 copy-start.4

commit v2 on v1

--- a/solution.py
+++ b/solution.py
@@ -9,7 +9,7 @@
 
 K = 8192
 NB = 4
-CHUNK = 64
+CHUNK = 128
 AHEAD = 2
 MESH = pl.DeviceIdType.MESH
 NT = (((1,), (1,)), ((), ()))
@@ -25,8 +25,8 @@
 
 
 def score_kernel(
-    n_row, n_dim, train_hbm, precond_ref, slot_hbm, raw_ref, g_ref, q_ref,
-    train, slot, blocks, parts, landed, g_out, g_in, q_out, q_in, q_sum, q_all,
+    n_row, n_dim, owner_ref, order_ref, train_hbm, precond_hbm, slot_hbm, out_ref,
+    raw_ref, column, q_ref, train, precond_ref, slot, blocks, parts, landed, g_out, g_in, q_out, q_in, q_sum, q_all,
     load_sem, hop_send, hop_recv, part_send, part_recv, norm_send, norm_recv, q_send, q_recv,
 ):
     z = lax.axis_index("row")
@@ -35,10 +35,11 @@
     queries = slot.shape[0]
     share = rows // n_dim
     steps = queries // CHUNK
-    half = 2 * CHUNK
 
     load_slot = pltpu.make_async_copy(slot_hbm, slot, load_sem.at[0])
     load_train = pltpu.make_async_copy(train_hbm, train, load_sem.at[1])
+    load_precond = pltpu.make_async_copy(precond_hbm, precond_ref, load_sem.at[2])
+    load_precond.start()
     load_slot.start()
     load_train.start()
 
@@ -62,7 +63,7 @@
     def send_part(b, c, r):
         to = lax.rem(d + r, n_dim)
         return pltpu.make_async_remote_copy(
-            src_ref=parts.at[b, to, rows_of(c)], dst_ref=landed.at[b, d, rows_of(c)],
+            src_ref=parts.at[b, c, to], dst_ref=landed.at[b, c, d],
             send_sem=part_send.at[b, r, c], recv_sem=part_recv.at[b, r, c],
             device_id={"dim": to}, device_id_type=MESH,
         )
@@ -79,20 +80,18 @@
         for r in PART_ORDER(n_dim):
             to = lax.rem(d + r, n_dim)
             mine = train[pl.ds(pl.multiple_of(to * share, share), share), :]
-            part = lax.dot_general(weighted, mine, NT, preferred_element_type=jnp.float32)
-            parts[b, to, rows_of(c), :] = part.astype(jnp.bfloat16)
+            part = lax.dot_general(mine, weighted, NT, preferred_element_type=jnp.float32)
+            parts[b, c, to] = part.astype(jnp.bfloat16)
             if r:
                 send_part(b, c, r).start()
 
-    def add_up(b, which):
-        for k in range(2):
-            for r in range(1, n_dim):
-                send_part(b, which * 2 + k, r).wait_recv()
-        at = pl.ds(which * half, half)
-        total = parts[b, d, at, :].astype(jnp.float32)
+    def add_up(b, c):
         for r in range(1, n_dim):
-            total = total + landed[b, lax.rem(d + r, n_dim), at, :].astype(jnp.float32)
-        raw_ref[b, :, at] = total.T
+            send_part(b, c, r).wait_recv()
+        total = parts[b, c, d].astype(jnp.float32)
+        for r in range(1, n_dim):
+            total = total + landed[b, c, lax.rem(d + r, n_dim)].astype(jnp.float32)
+        raw_ref[b, c] = total
 
     def each_block(h, run):
         if h == 0:
@@ -101,6 +100,7 @@
             pl.when(z - h >= 0)(lambda: run(z - h))
             pl.when(z + h < n_row)(lambda: run(z + h))
 
+    load_precond.wait()
     load_slot.wait()
     for c in range(AHEAD):
         weigh(c)
@@ -152,11 +152,9 @@
             if h == 1:
                 pl.when(c + AHEAD < steps)(lambda: send_own(c + AHEAD))
             each_block(h, lambda b: product(b, c))
-            for which in range(steps // 2):
-                if which == 0:
-                    pl.when(c == 0)(lambda: each_block(h - 1, lambda b: add_up(b, steps // 2 - 1)) if h > 1 else None)
-                else:
-                    pl.when(c == 2 * which)(lambda which=which: each_block(h, lambda b: add_up(b, which - 1)))
+            if h > 1:
+                pl.when(c == 0)(lambda: each_block(h - 1, lambda b: add_up(b, steps - 1)))
+            pl.when(c > 0)(lambda: each_block(h, lambda b: add_up(b, c - 1)))
             if h == 1:
                 pl.when(c < n_dim)(lambda: train_norms(c))
             return carry
@@ -173,24 +171,31 @@
             for r in range(1, n_dim):
                 total = total + q_in[lax.rem(d + r, n_dim)]
             q_sum[...] = total
-            q_ref[z] = total
+            q_ref[z] = lax.rsqrt(total / K + 1e-06)
             for r in range(1, n_row):
                 q_copy(r).start()
-            for which in range(steps // 2):
-                add_up(z, which)
+            for c in range(steps):
+                add_up(z, c)
             for r in range(1, n_dim):
                 norm_copy(r, 0).wait_recv()
             total = g_out[d]
             for r in range(1, n_dim):
                 total = total + g_in[lax.rem(d + r, n_dim)]
-            g_ref[...] = total
+            g = lax.rsqrt(K * (total[0:1, :] / K + 1e-06))
+            column[...] = jnp.broadcast_to(g, (128, share)).T
         if h == 2:
             for r in range(1, n_row):
                 q_copy(r).wait_recv()
             for r in range(1, n_row):
                 other = lax.rem(z + r, n_row)
-                q_ref[other] = q_all[other]
-    each_block(n_row - 1, lambda b: add_up(b, steps // 2 - 1))
+                q_ref[other] = lax.rsqrt(q_all[other] / K + 1e-06)
+    each_block(n_row - 1, lambda b: add_up(b, steps - 1))
+    for s in range(NB):
+        root = owner_ref[order_ref[s]]
+        q = q_ref[root]
+        for c in range(steps):
+            at = slice(c * CHUNK, (c + 1) * CHUNK)
+            out_ref[s, :, at] = raw_ref[root, c] * column[...] * q[0:1, at]
 
     def sent(c, carry):
         for b in range(n_row):
@@ -213,37 +218,38 @@
     return [middle] + [r for r in range(1, n_dim) if r != middle] + [0]
 
 
-def raw_scores(n_row, n_dim, train_grads, precond, slot):
+def scores(n_row, n_dim, owner, order, train_grads, precond, slot):
     rows, width = train_grads.shape
     queries = slot.shape[0]
     share = rows // n_dim
     steps = queries // CHUNK
     f32, bf16 = jnp.float32, jnp.bfloat16
     vmem = pl.BlockSpec(memory_space=pltpu.VMEM)
-    anywhere = pl.BlockSpec(memory_space=pl.ANY)
+    hbm = pl.BlockSpec(memory_space=pltpu.HBM)
+    smem = pl.BlockSpec(memory_space=pltpu.SMEM)
     dma = pltpu.SemaphoreType.DMA
     return pl.pallas_call(
         functools.partial(score_kernel, n_row, n_dim),
-        out_shape=(
-            jax.ShapeDtypeStruct((n_row, share, queries), f32),
-            jax.ShapeDtypeStruct((8, share), f32),
-            jax.ShapeDtypeStruct((n_row, 8, queries), f32),
-        ),
-        in_specs=[anywhere, vmem, anywhere],
-        out_specs=(vmem, vmem, vmem),
+        out_shape=jax.ShapeDtypeStruct((NB, share, queries), f32),
+        in_specs=[smem, smem, hbm, hbm, hbm],
+        out_specs=vmem,
         scratch_shapes=[
+            pltpu.VMEM((n_row, steps, share, CHUNK), f32),
+            pltpu.VMEM((share, 128), f32),
+            pltpu.VMEM((n_row, 8, queries), f32),
             pltpu.VMEM((rows, width), bf16),
+            pltpu.VMEM((1, width), f32),
             pltpu.VMEM((queries, width), bf16),
             pltpu.VMEM((n_row, queries, width), bf16),
-            pltpu.VMEM((n_row, n_dim, queries, share), bf16),
-            pltpu.VMEM((n_row, n_dim, queries, share), bf16),
+            pltpu.VMEM((n_row, steps, n_dim, share, CHUNK), bf16),
+            pltpu.VMEM((n_row, steps, n_dim, share, CHUNK), bf16),
             pltpu.VMEM((n_dim, 8, share), f32),
             pltpu.VMEM((n_dim, 8, share), f32),
             pltpu.VMEM((8, queries), f32),
             pltpu.VMEM((n_dim, 8, queries), f32),
             pltpu.VMEM((8, queries), f32),
             pltpu.VMEM((n_row, 8, queries), f32),
-            dma((2,)),
+            dma((3,)),
             dma((2, n_row, steps)),
             dma((n_row, steps)),
             dma((n_row, n_dim, steps)),
@@ -256,42 +262,12 @@
         compiler_params=pltpu.CompilerParams(
             collective_id=0, has_side_effects=True, vmem_limit_bytes=48 * 1024 * 1024
         ),
-        name="scores_raw",
-    )(train_grads, precond.reshape(1, width), slot)
-
-
-def normalise_kernel(owner, order, raw_ref, g_ref, q_ref, out_ref):
-    queries = raw_ref.shape[2]
-    share = raw_ref.shape[1]
-    g = lax.rsqrt(K * (g_ref[0:1, :] / K + 1e-06))
-    column = jnp.broadcast_to(g, (128, share)).T
-    q = lax.rsqrt(q_ref[0, 0:1, :] / K + 1e-06)
-    for at in range(0, queries, 128):
-        out_ref[0, :, at : at + 128] = raw_ref[0, :, at : at + 128] * column * q[:, at : at + 128]
-
-
-def normalise(raw, g, q, owner, order):
-    n, share, queries = raw.shape
-    return pl.pallas_call(
-        normalise_kernel,
-        out_shape=jax.ShapeDtypeStruct((NB, share, queries), jnp.float32),
-        grid_spec=pltpu.PrefetchScalarGridSpec(
-            num_scalar_prefetch=2,
-            grid=(NB,),
-            in_specs=[
-                pl.BlockSpec((1, share, queries), lambda s, owner, order: (owner[order[s]], 0, 0)),
-                pl.BlockSpec((8, share), lambda s, owner, order: (0, 0)),
-                pl.BlockSpec((1, 8, queries), lambda s, owner, order: (owner[order[s]], 0, 0)),
-            ],
-            out_specs=pl.BlockSpec((1, share, queries), lambda s, owner, order: (s, 0, 0)),
-        ),
-        name="normalise",
-    )(owner, order, raw, g, q)
+        name="scores",
+    )(owner, order, train_grads, precond.reshape(1, width), slot)
 
 
 def every_slot(train_grads, precond, query_store, owner, order):
-    raw, g, q = raw_scores(lax.axis_size("row"), lax.axis_size("dim"), train_grads, precond, query_store[0])
-    return normalise(raw, g, q, owner, order)
+    return scores(lax.axis_size("row"), lax.axis_size("dim"), owner, order, train_grads, precond, query_store[0])
 
 
 def weighted_norm(values, precond):

time: 89.5 us -> 85.4 us (0.954)
  Pallas kernels: 85.1 us -> 80.9 us
    pallas_call x2 -> x1, Pallas kernels: 85.1 us -> 80.9 us  [scores(): pl.pallas_call(functools.partial(score_kernel, n_row, n_dim), out_shape=j...]
    unnamed x10 -> x9, local copies, waits for them, and re-layouts: 4.08 us -> 4.2 us
where the time goes in v2:
time: 85.4 us; the launch traced here: 85.1 us
  Pallas kernels  80.9 us (95%)
  local copies, waits for them, and re-layouts  4.2 us (5%)
    pallas_call x1, Pallas kernels, scores(): pl.pallas_call(functools.partial(score_kernel, n_row, n_dim), out_shape=j...  80.9 us
    unnamed x9, local copies, waits for them, and re-layouts  4.2 us

profile of v2, /device:TPU:1, one launch (start us, length us, event | category | flops | bytes accessed | tf_op | source)
XLA Modules:
  0.0 85.1 jit_solution(7322339336997873441)
XLA Ops:
  0.0 0.0 copy-start
  0.0 1.2 %copy-done = bf16[1,256,2048]{2,1,0:T(8,128)(2,1)S(1)} copy-done((bf16[1,256,2048]{2,1,0:T(8,128)(2,1)S(1)}, bf16[1,256,2048]{2,1,0:T(8,128)(2,1)}, u32[]{:S(2)}) %copy-start) | copy-done | bytes 1048600
  1.2 0.0 copy-start.1
  1.2 0.7 copy-done.1
  1.9 0.0 copy-start.2
  1.9 0.7 copy-done.2
  2.6 0.0 copy-start.3
  2.6 0.7 copy-done.3
  3.2 80.9 %scores.1 = f32[4,256,256]{2,1,0:T(8,128)S(1)} custom-call(s32[4]{0:T(128)S(1)} %copy-done.2, s32[4]{0:T(128)S(1)} %copy-done.3, bf16[1024,2048]{1,0:T(8,128)(2,1)} %train_hbm.1, f32[1,2048]{1,0:T(1,128)S(1)} %bitcast.3, bf16[256,2048]{1,0:T(8,128)(2,1)S(1)} %bitcast.2), custom_call_target="tpu_custom_call" | custom-call | tf_op jit(solution)/shard_map/scores/pallas_call | solution.py:231
  84.2 1.0 %copy.7 = f32[4,256,256]{2,1,0:T(8,128)} copy(f32[4,256,256]{2,1,0:T(8,128)S(1)} %scores.1) | data formatting | bytes 2097152
Async XLA Ops:
  0.0 1.2 %copy-start = (bf16[1,256,2048]{2,1,0:T(8,128)(2,1)S(1)}, bf16[1,256,2048]{2,1,0:T(8,128)(2,1)}, u32[]{:S(2)}) copy-start(bf16[1,256,2048]{2,1,0:T(8,128)(2,1)} %param.7) | copy-start | bytes 3145732
  1.2 0.7 copy-start.1
  1.9 0.7 copy-start.2
  2.6 0.7 copy-start.3

commit v3 on v2

--- a/solution.py
+++ b/solution.py
@@ -11,6 +11,7 @@
 NB = 4
 CHUNK = 128
 AHEAD = 2
+VMEM_MIB = 63
 MESH = pl.DeviceIdType.MESH
 NT = (((1,), (1,)), ((), ()))
 
@@ -25,8 +26,8 @@
 
 
 def score_kernel(
-    n_row, n_dim, owner_ref, order_ref, train_hbm, precond_hbm, slot_hbm, out_ref,
-    raw_ref, column, q_ref, train, precond_ref, slot, blocks, parts, landed, g_out, g_in, q_out, q_in, q_sum, q_all,
+    n_row, n_dim, owner_hbm, order_hbm, train_hbm, precond_hbm, slot_hbm, out_ref,
+    owner_ref, order_ref, raw_ref, column, q_ref, train, precond_ref, slot, blocks, parts, landed, g_out, g_in, q_out, q_in, q_sum, q_all,
     load_sem, hop_send, hop_recv, part_send, part_recv, norm_send, norm_recv, q_send, q_recv,
 ):
     z = lax.axis_index("row")
@@ -39,9 +40,13 @@
     load_slot = pltpu.make_async_copy(slot_hbm, slot, load_sem.at[0])
     load_train = pltpu.make_async_copy(train_hbm, train, load_sem.at[1])
     load_precond = pltpu.make_async_copy(precond_hbm, precond_ref, load_sem.at[2])
+    load_owner = pltpu.make_async_copy(owner_hbm, owner_ref, load_sem.at[3])
+    load_order = pltpu.make_async_copy(order_hbm, order_ref, load_sem.at[4])
     load_precond.start()
     load_slot.start()
     load_train.start()
+    load_owner.start()
+    load_order.start()
 
     barrier = pltpu.get_barrier_semaphore()
     for r in range(1, n_row):
@@ -190,6 +195,8 @@
                 other = lax.rem(z + r, n_row)
                 q_ref[other] = lax.rsqrt(q_all[other] / K + 1e-06)
     each_block(n_row - 1, lambda b: add_up(b, steps - 1))
+    load_owner.wait()
+    load_order.wait()
     for s in range(NB):
         root = owner_ref[order_ref[s]]
         q = q_ref[root]
@@ -226,14 +233,15 @@
     f32, bf16 = jnp.float32, jnp.bfloat16
     vmem = pl.BlockSpec(memory_space=pltpu.VMEM)
     hbm = pl.BlockSpec(memory_space=pltpu.HBM)
-    smem = pl.BlockSpec(memory_space=pltpu.SMEM)
     dma = pltpu.SemaphoreType.DMA
     return pl.pallas_call(
         functools.partial(score_kernel, n_row, n_dim),
         out_shape=jax.ShapeDtypeStruct((NB, share, queries), f32),
-        in_specs=[smem, smem, hbm, hbm, hbm],
+        in_specs=[hbm, hbm, hbm, hbm, hbm],
         out_specs=vmem,
         scratch_shapes=[
+            pltpu.SMEM((NB,), jnp.int32),
+            pltpu.SMEM((NB,), jnp.int32),
             pltpu.VMEM((n_row, steps, share, CHUNK), f32),
             pltpu.VMEM((share, 128), f32),
             pltpu.VMEM((n_row, 8, queries), f32),
@@ -249,7 +257,7 @@
             pltpu.VMEM((n_dim, 8, queries), f32),
             pltpu.VMEM((8, queries), f32),
             pltpu.VMEM((n_row, 8, queries), f32),
-            dma((3,)),
+            dma((5,)),
             dma((2, n_row, steps)),
             dma((n_row, steps)),
             dma((n_row, n_dim, steps)),
@@ -260,7 +268,7 @@
             dma((n_row,)),
         ],
         compiler_params=pltpu.CompilerParams(
-            collective_id=0, has_side_effects=True, vmem_limit_bytes=48 * 1024 * 1024
+            collective_id=0, has_side_effects=True, vmem_limit_bytes=VMEM_MIB * 1024 * 1024
         ),
         name="scores",
     )(owner, order, train_grads, precond.reshape(1, width), slot)

time: 85.4 us -> 83.8 us (0.981)
  local copies, waits for them, and re-layouts: 4.2 us -> 2.29 us
    unnamed x9 -> x1, local copies, waits for them, and re-layouts: 4.2 us -> 2.29 us
where the time goes in v3:
time: 83.8 us; the launch traced here: 83.6 us
  Pallas kernels  81.3 us (97%)
  local copies, waits for them, and re-layouts  2.29 us (3%)
    pallas_call x1, Pallas kernels, scores(): pl.pallas_call(functools.partial(score_kernel, n_row, n_dim), out_shape=j...  81.3 us
    unnamed x1, local copies, waits for them, and re-layouts  2.29 us

profile of v3, /device:TPU:1, one launch (start us, length us, event | category | flops | bytes accessed | tf_op | source)
XLA Modules:
  0.0 83.6 jit_solution(2036966187419723937)
XLA Ops:
  0.0 81.3 %scores.1 = f32[4,256,256]{2,1,0:T(8,128)} custom-call(s32[4]{0:T(128)} %owner_hbm.1, s32[4]{0:T(128)} %order_hbm.1, bf16[1024,2048]{1,0:T(8,128)(2,1)} %train_hbm.1, f32[1,2048]{1,0:T(1,128)} %bitcast.3, bf16[256,2048]{1,0:T(8,128)(2,1)} %bitcast.2), custom_call_target="tpu_custom_call" | custom-call | tf_op jit(solution)/shard_map/scores/pallas_call | solution.py:237
  81.3 2.3 %copy.7 = f32[4,256,256]{2,1,0:T(8,128)} copy(f32[4,256,256]{2,1,0:T(8,128)} %scores.1) | data formatting | bytes 2097152
